TPU v7x, 512 devices: a whole 4x4x16 slice. The times are simulated.
512 devices in a mesh: fsdp: 32 (over z, core), expert: 16 (over x, y).
Axes of the slice: x: 4, y: 4, z: 16, core: 2. Of those that a mesh axis runs over, the one named last changes fastest.
Arguments:
- tokens: bfloat16 [65536, 4096], P(('fsdp', 'expert')), may hold values from -6 to 6
- expert_ids: int32 [65536, 2], P(('fsdp', 'expert')), may hold values from 0 to 15, all different within a row
- gate_probs: float32 [65536, 2], P(('fsdp', 'expert')), may hold values from 0.1 to 1
- up_weight: bfloat16 [16, 4096, 768], P('expert', 'fsdp'), may hold values from -0.09375 to 0.09375
- down_weight: bfloat16 [16, 768, 4096], P('expert', None, 'fsdp'), may hold values from -0.21875 to 0.21875
- out_grad: bfloat16 [65536, 4096], P(('fsdp', 'expert')), may hold values from -6 to 6
Outputs:
- d_tokens: bfloat16 [65536, 4096], P(('fsdp', 'expert'))
- d_gates: bfloat16 [65536, 2], P(('fsdp', 'expert'))
Inputs may be any that keep to these rules, and one draw needn't show every extreme that they name: `expert_ids`: each token names two different experts, and every expert is named by some token.
All inputs are finite; a program needn't handle non-finite values.
Results may differ from a plain program's by a relative error of at most 0.017.
Values may be sent and summed in bfloat16 or wider, within the bound.
No kernel may reach another device: no remote copies, remote signals or barrier semaphores. Data moves between devices by JAX's collectives and lax.ppermute only.
A program may use at most 64 MiB of HBM per device.

v0:
```python
import jax
import jax.numpy as jnp
from jax import lax
from jax.sharding import PartitionSpec as P


def gelu_parts(hidden):
    normal_cdf = 0.5 * (1.0 + lax.erf(hidden * 0.7071067811865476))
    density = jnp.exp(-0.5 * hidden * hidden) * 0.3989422804014327
    return (hidden * normal_cdf, normal_cdf + hidden * density)


def right_product(left, right):
    return lax.dot_general(
        left, right, (((1,), (1,)), ((), ())), preferred_element_type=jnp.float32
    )


def body(tokens, expert_ids, gate_probs, up_weight, down_weight, out_grad):
    experts = lax.axis_size("expert")
    token_count = tokens.shape[0]
    width = tokens.shape[1]
    capacity = 3 * token_count // (2 * experts)
    slot_count = experts * capacity
    flat_ids = expert_ids.reshape(-1)
    onehot = (flat_ids[:, None] == jnp.arange(experts, dtype=jnp.int32)[None, :]).astype(jnp.int32)
    position = jnp.sum((jnp.cumsum(onehot, axis=0) - 1) * onehot, axis=1)
    kept_mask = position < capacity
    slot_index = flat_ids * capacity + jnp.minimum(position, capacity - 1)
    target = jnp.where(kept_mask, slot_index, slot_count)
    match_rows = (jnp.arange(slot_count, dtype=jnp.int32)[:, None] == target[None, :]).astype(
        jnp.bfloat16
    )
    match_rows = match_rows.reshape(slot_count, token_count, 2).sum(axis=2)
    send_tokens = (
        jnp.dot(match_rows, tokens, preferred_element_type=jnp.float32)
        .astype(jnp.bfloat16)
        .reshape(experts, capacity, width)
    )
    send_grads = (
        jnp.dot(match_rows, out_grad, preferred_element_type=jnp.float32)
        .astype(jnp.bfloat16)
        .reshape(experts, capacity, width)
    )
    recv_tokens, recv_grads = (
        lax.all_to_all(send_tokens, "expert", split_axis=0, concat_axis=0, tiled=True),
        lax.all_to_all(send_grads, "expert", split_axis=0, concat_axis=0, tiled=True),
    )
    flat_tokens = recv_tokens.reshape(slot_count, width)
    up_full, down_full = (
        lax.all_gather(up_weight, "fsdp", axis=1, tiled=True),
        lax.all_gather(down_weight, "fsdp", axis=2, tiled=True),
    )
    up_matrix = up_full[0]
    hidden = jnp.dot(flat_tokens, up_matrix, preferred_element_type=jnp.float32)
    value, slope = gelu_parts(hidden)
    active = value.astype(jnp.bfloat16)
    flat_grads = recv_grads.reshape(slot_count, width)
    active_grad = right_product(flat_grads, down_full[0])
    gate_grad = jnp.sum(active.astype(jnp.float32) * active_grad, axis=1).astype(jnp.bfloat16)
    hidden_grad = (active_grad * slope).astype(jnp.bfloat16)
    input_grad = right_product(hidden_grad, up_matrix).astype(jnp.bfloat16)
    back_inputs, back_gates = (
        lax.all_to_all(
            input_grad.reshape(experts, capacity, width),
            "expert",
            split_axis=0,
            concat_axis=0,
            tiled=True,
        ),
        lax.all_to_all(
            gate_grad.reshape(experts, capacity), "expert", split_axis=0, concat_axis=0, tiled=True
        ),
    )
    picked = back_inputs.reshape(slot_count, width)[slot_index]
    weight = jnp.where(kept_mask, gate_probs.reshape(-1), 0.0)
    terms = (picked.astype(jnp.float32) * weight[:, None]).reshape(token_count, 2, width)
    d_tokens = (terms[:, 0, :] + terms[:, 1, :]).astype(jnp.bfloat16)
    d_gates = jnp.where(kept_mask, back_gates.reshape(-1)[slot_index], 0).reshape(token_count, 2)
    return (d_tokens, d_gates)


def solution(mesh):
    placed = (
        P(("fsdp", "expert"), None),
        P(("fsdp", "expert"), None),
        P(("fsdp", "expert"), None),
        P("expert", "fsdp", None),
        P("expert", None, "fsdp"),
        P(("fsdp", "expert"), None),
    )
    return jax.shard_map(
        body,
        mesh=mesh,
        in_specs=placed,
        out_specs=(P(("fsdp", "expert"), None), P(("fsdp", "expert"), None)),
        check_vma=False,
    )
```

profile of v0, /device:TPU:1, one launch (start us, length us, event | category | flops | bytes accessed | tf_op | source)
XLA Modules:
  0.0 257.6 jit_solution(20404745046377142)
XLA Ops:
  7.2 0.0 copy-start
  7.2 0.0 all-gather.5.cloned.1.call-start
  7.2 0.7 all-gather.5.cloned.1.call-update
  7.9 0.0 all-gather.3.cloned.1.call-start
  8.0 0.7 all-gather.3.cloned.1.call-update
  8.7 0.8 copy.27
  9.4 0.1 eq.44
  9.6 0.1 eq.40
  9.7 0.6 reduce-window.6
  10.3 0.2 slice_reduce_fusion
  10.6 0.1 fusion.23
  10.7 0.2 lt.27
  10.8 0.1 min.25
  11.0 0.1 copy.31
  11.1 0.0 copy-done
  11.1 0.6 convolution_convert_fusion
  11.7 1.5 reshape.144
  13.2 7.6 %all-to-all-start.1 = ((bf16[16,12,4096]{2,1,0:T(8,128)(2,1)}), bf16[16,12,4096]{2,1,0:T(8,128)(2,1)S(1)}, u32[]{:S(2)}, u32[]{:S(2)}) async-start(bf16[16,12,4096]{2,1,0:T(8,128)(2,1)} %reshape.144), calls=%async_computation.1 | async-start | bytes 4194304 | tf_op jit(solution)/shard_map/all_to_all | solution.py:46
  20.8 2.9 %convolution_convert_fusion.1 = bf16[192,4096]{1,0:T(8,128)(2,1)} fusion(bf16[192,128]{1,0:T(8,128)(2,1)S(1)} %fusion.21, bf16[128,4096]{1,0:T(8,128)(2,1)} %param.11), kind=kOutput, calls=%fused_computation.10 | convolution fusion | flops 202113024 | bytes 2670592 | tf_op jit(solution)/shard_map/dot_general | solution.py:41
  23.8 3.4 %reshape.142 = bf16[16,12,4096]{2,1,0:T(8,128)(2,1)} reshape(bf16[192,4096]{1,0:T(8,128)(2,1)} %convolution_convert_fusion.1) | data formatting | bytes 3145728 | tf_op jit(solution)/shard_map/reshape | solution.py:43
  27.2 19.0 %all-to-all-done.1 = bf16[16,12,4096]{2,1,0:T(8,128)(2,1)S(1)} async-done(((bf16[16,12,4096]{2,1,0:T(8,128)(2,1)}), bf16[16,12,4096]{2,1,0:T(8,128)(2,1)S(1)}, u32[]{:S(2)}, u32[]{:S(2)}) %all-to-all-start.1) | async-done | bytes 1572896 | tf_op jit(solution)/shard_map/all_to_all | solution.py:46
  46.1 6.5 %all-to-all-start = ((bf16[16,12,4096]{2,1,0:T(8,128)(2,1)}), bf16[16,12,4096]{2,1,0:T(8,128)(2,1)}, u32[]{:S(2)}, u32[]{:S(2)}) async-start(bf16[16,12,4096]{2,1,0:T(8,128)(2,1)} %reshape.142), calls=%async_computation | async-start | bytes 4194304 | tf_op jit(solution)/shard_map/all_to_all | solution.py:47
  52.7 1.4 reshape.145
  54.0 23.8 %all-to-all-done = bf16[16,12,4096]{2,1,0:T(8,128)(2,1)} async-done(((bf16[16,12,4096]{2,1,0:T(8,128)(2,1)}), bf16[16,12,4096]{2,1,0:T(8,128)(2,1)}, u32[]{:S(2)}, u32[]{:S(2)}) %all-to-all-start) | async-done | bytes 1572896 | tf_op jit(solution)/shard_map/all_to_all | solution.py:47
  77.9 2.5 reshape.143
  80.3 12.6 %all-gather.5.cloned.1.call-done = bf16[1,4096,768]{2,1,0:T(8,128)(2,1)} async-done(((bf16[1,128,768]{2,1,0:T(8,128)(2,1)}), bf16[1,4096,768]{2,1,0:T(8,128)(2,1)}) %all-gather.5.cloned.1.call-update) | async-done | bytes 6291472 | tf_op jit(solution)/shard_map/all_gather | solution.py:51
  93.0 4.7 %fusion.2 = f32[192,768]{1,0:T(8,128)S(1)} fusion(bf16[192,4096]{1,0:T(8,128)(2,1)} %reshape.145, bf16[1,4096,768]{2,1,0:T(8,128)(2,1)} %all-gather.5.cloned.1.call-done), kind=kOutput, calls=%fused_computation.4 | convolution fusion | flops 1207959552 | bytes 8454144 | tf_op jit(solution)/shard_map/dot_general | solution.py:55
  97.6 82.8 %all-gather.3.cloned.1.call-done = bf16[1,768,4096]{2,1,0:T(8,128)(2,1)} async-done(((bf16[1,768,128]{2,1,0:T(8,128)(2,1)}), bf16[1,768,4096]{2,1,0:T(8,128)(2,1)}) %all-gather.3.cloned.1.call-update) | async-done | bytes 6291472 | tf_op jit(solution)/shard_map/all_gather | solution.py:52
  180.5 5.8 %multiply_reduce_fusion = (bf16[192]{0:T(256)(128)(2,1)S(1)}, f32[192,768]{1,0:T(8,128)}) fusion(f32[192,768]{1,0:T(8,128)S(1)} %fusion.2, bf16[192,4096]{1,0:T(8,128)(2,1)S(1)} %reshape.143, bf16[1,768,4096]{2,1,0:T(8,128)(2,1)} %all-gather.3.cloned.1.call-done), kind=kOutput, calls=%fused_computation.22 | convolution fusion | flops 1209138944 | bytes 9044352 | tf_op jit(solution)/shard_map/dot_general | solution.py:14
  186.3 0.7 convert_element_type.73
  187.0 6.5 %all-to-all-start.3 = ((bf16[16,1,12]{2,1,0:T(2,128)(2,1)}), bf16[16,1,12]{2,1,0:T(2,128)(2,1)S(1)}, u32[]{:S(2)}, u32[]{:S(2)}) async-start(bf16[16,1,12]{2,1,0:T(2,128)(2,1)} %convert_element_type.73), calls=%async_computation.3 | async-start | bytes 16384 | tf_op jit(solution)/shard_map/all_to_all | solution.py:71
  193.5 5.1 %fusion.6 = bf16[192,4096]{1,0:T(8,128)(2,1)S(1)} fusion(bf16[1,4096,768]{2,1,0:T(8,128)(2,1)} %all-gather.5.cloned.1.call-done, f32[192,768]{1,0:T(8,128)} %get-tuple-element.11, f32[192,768]{1,0:T(8,128)S(1)} %fusion.2), kind=kOutput, calls=%fused_computation.8 | convolution fusion | flops 1210220544 | bytes 9043968 | tf_op jit(solution)/shard_map/dot_general | solution.py:14
  198.7 1.6 reshape.146
  200.2 0.0 copy-start.1
  200.2 0.0 all-to-all-done.3
  200.2 6.8 %all-to-all-start.2 = ((bf16[16,12,4096]{2,1,0:T(8,128)(2,1)}), bf16[16,12,4096]{2,1,0:T(8,128)(2,1)}, u32[]{:S(2)}, u32[]{:S(2)}) async-start(bf16[16,12,4096]{2,1,0:T(8,128)(2,1)} %reshape.146), calls=%async_computation.2 | async-start | bytes 4194304 | tf_op jit(solution)/shard_map/all_to_all | solution.py:64
  207.1 0.1 mul.81
  207.2 0.0 copy-done.1
  207.2 0.1 copy.32
  207.3 0.1 copy.33
  207.5 0.1 reshape.148
  207.6 1.9 gather_fusion.1
  209.5 0.2 gather.10
  209.6 0.6 copy.36
  210.2 23.6 %all-to-all-done.2 = bf16[16,12,4096]{2,1,0:T(8,128)(2,1)} async-done(((bf16[16,12,4096]{2,1,0:T(8,128)(2,1)}), bf16[16,12,4096]{2,1,0:T(8,128)(2,1)}, u32[]{:S(2)}, u32[]{:S(2)}) %all-to-all-start.2) | async-done | bytes 1572896 | tf_op jit(solution)/shard_map/all_to_all | solution.py:64
  233.8 2.5 reshape.147
  236.3 3.2 %gather_fusion = bf16[256,4096]{1,0:T(8,128)(2,1)} fusion(bf16[192,4096]{1,0:T(8,128)(2,1)S(1)} %reshape.147, s32[1024]{0:T(1024)S(1)} %pad_clamp_fusion), kind=kCustom, calls=%fused_computation | custom fusion | bytes 4195328 | tf_op jit(solution)/shard_map/gather | solution.py:75
  239.5 5.4 %reshape.149 = f32[128,2,4096]{2,1,0:T(2,128)} reshape(bf16[256,4096]{1,0:T(8,128)(2,1)} %gather_fusion) | data formatting | bytes 6291456 | tf_op jit(solution)/shard_map/convert_element_type | solution.py:77
  244.9 4.6 %copy_multiply_fusion = f32[128,2,4096]{2,0,1:T(8,128)S(1)} fusion(f32[128,2,4096]{2,1,0:T(2,128)} %reshape.149, f32[128,2]{0,1:T(2,128)S(1)} %copy.33), kind=kLoop, calls=%fused_computation.11 | loop fusion | flops 1048576 | bytes 8389632 | tf_op jit(solution)/shard_map/mul | solution.py:77
  249.6 1.2 fusion.10
  (12 shorter events, 0.2 us)
Async XLA Ops:
  7.2 4.0 %copy-start = (bf16[128,4096]{1,0:T(8,128)(2,1)S(1)}, bf16[128,4096]{1,0:T(8,128)(2,1)}, u32[]{:S(2)}) copy-start(bf16[128,4096]{1,0:T(8,128)(2,1)} %param.6) | copy-start | bytes 3145732
  7.2 85.8 %all-gather.5.cloned.1.call-start = ((), (), s32[]{:S(2)}) async-start(), calls=%async_computation.5 | async-start | bytes 6488064 | tf_op jit(solution)/shard_map/all_gather | solution.py:51
  7.9 172.6 %all-gather.3.cloned.1.call-start = ((), (), s32[]{:S(2)}) async-start(), calls=%async_computation.4 | async-start | bytes 6488064 | tf_op jit(solution)/shard_map/all_gather | solution.py:52
  13.2 32.9 %all-to-all-start.1 = ((bf16[16,12,4096]{2,1,0:T(8,128)(2,1)}), bf16[16,12,4096]{2,1,0:T(8,128)(2,1)S(1)}, u32[]{:S(2)}, u32[]{:S(2)}) async-start(bf16[16,12,4096]{2,1,0:T(8,128)(2,1)} %reshape.144), calls=%async_computation.1 | async-start | bytes 4194304 | tf_op jit(solution)/shard_map/all_to_all | solution.py:46
  46.1 31.7 %all-to-all-start = ((bf16[16,12,4096]{2,1,0:T(8,128)(2,1)}), bf16[16,12,4096]{2,1,0:T(8,128)(2,1)}, u32[]{:S(2)}, u32[]{:S(2)}) async-start(bf16[16,12,4096]{2,1,0:T(8,128)(2,1)} %reshape.142), calls=%async_computation | async-start | bytes 4194304 | tf_op jit(solution)/shard_map/all_to_all | solution.py:47
  187.0 13.2 %all-to-all-start.3 = ((bf16[16,1,12]{2,1,0:T(2,128)(2,1)}), bf16[16,1,12]{2,1,0:T(2,128)(2,1)S(1)}, u32[]{:S(2)}, u32[]{:S(2)}) async-start(bf16[16,1,12]{2,1,0:T(2,128)(2,1)} %convert_element_type.73), calls=%async_computation.3 | async-start | bytes 16384 | tf_op jit(solution)/shard_map/all_to_all | solution.py:71
  200.2 7.0 %copy-start.1 = (f32[128,2]{0,1:T(2,128)S(1)}, f32[128,2]{0,1:T(2,128)}, u32[]{:S(2)}) copy-start(f32[128,2]{0,1:T(2,128)} %param.8) | copy-start | bytes 3076
  200.2 33.6 %all-to-all-start.2 = ((bf16[16,12,4096]{2,1,0:T(8,128)(2,1)}), bf16[16,12,4096]{2,1,0:T(8,128)(2,1)}, u32[]{:S(2)}, u32[]{:S(2)}) async-start(bf16[16,12,4096]{2,1,0:T(8,128)(2,1)} %reshape.146), calls=%async_computation.2 | async-start | bytes 4194304 | tf_op jit(solution)/shard_map/all_to_all | solution.py:64
Sparse Core Ops, SparseCore 0:
  10.1 82.8 all-gather.4
  95.0 85.3 all-gather.2
where the time goes:
time: 260 us; the launch traced here: 258 us
  waiting for transfers between devices  163 us (63%)
  starting transfers between devices  27.6 us (11%)
  local copies, waits for them, and re-layouts  26.7 us (10%)
  matrix products  19.1 us (7%)
  between operations  14.2 us (5%)
  other arithmetic  6.7 us (3%)
    all_gather x1, waiting for transfers between devices, body(): lax.all_gather(down_weight, 'fsdp', axis=2, tiled=True)  82.8 us
    all_to_all x1, waiting for transfers between devices, body(): lax.all_to_all(send_grads, 'expert', split_axis=0, concat_axis=0, tiled=T...  23.8 us
    all_to_all x1, waiting for transfers between devices, body(): lax.all_to_all(input_grad.reshape(experts, capacity, width), 'expert', sp...  23.6 us
    all_to_all x1, waiting for transfers between devices, body(): lax.all_to_all(send_tokens, 'expert', split_axis=0, concat_axis=0, tiled=...  19 us
    all_gather x1, waiting for transfers between devices, body(): lax.all_gather(up_weight, 'fsdp', axis=1, tiled=True)  12.6 us
    dot_general x2, matrix products, right_product(): lax.dot_general(left, right, (((1,), (1,)), ((), ())), preferred_element_...  11 us
    all_to_all x1, starting transfers between devices, body(): lax.all_to_all(send_tokens, 'expert', split_axis=0, concat_axis=0, tiled=...  7.58 us
    all_to_all x1, starting transfers between devices, body(): lax.all_to_all(input_grad.reshape(experts, capacity, width), 'expert', sp...  6.85 us
  transfers between devices with their start and end apart: 6, of which 5 were waited for; matrix products, arithmetic and copies ran while one was open for 11% of the time, Pallas kernels for 0%

commit v1 on v0

v1 whole, which is shorter than its diff:
```python
import functools

import jax
import jax.numpy as jnp
from jax import lax
from jax.experimental import pallas as pl
from jax.experimental.pallas import tpu as pltpu
from jax.sharding import PartitionSpec as P

F32, BF16 = jnp.float32, jnp.bfloat16
VMEM_LIMIT = 56 * 1024 * 1024


def dot(left, right):
    return jnp.dot(left, right, preferred_element_type=F32)


def dot_t(left, right):
    return lax.dot_general(left, right, (((1,), (1,)), ((), ())), preferred_element_type=F32)


def iota(shape, axis):
    return lax.broadcasted_iota(jnp.int32, shape, axis)


def params(*semantics):
    return pltpu.CompilerParams(dimension_semantics=semantics, vmem_limit_bytes=VMEM_LIMIT)


def slot_table(ids, experts, capacity):
    tokens = ids.shape[1]
    expert = iota((experts, tokens), 0)
    named = (expert == ids[0:1, :]) | (expert == ids[1:2, :])
    before = (iota((tokens, tokens), 0) < iota((tokens, tokens), 1)).astype(F32).astype(BF16)
    count = dot(named.astype(F32).astype(BF16), before)
    return jnp.where(named & (count < capacity), count, -1.0)


def dispatch_kernel(experts, capacity, ids_ref, gates_ref, tl, th, gl, gh, send_ref, mix_ref, own_ref, pick):
    rows = 2 * capacity
    tokens = ids_ref.shape[1]

    @pl.when(pl.program_id(0) == 0)
    def _():
        ids = ids_ref[...]
        table = slot_table(ids, experts, capacity)
        count = experts * rows
        spread = (iota((count, experts), 0) // rows == iota((count, experts), 1)).astype(F32).astype(BF16)
        place = iota((count, tokens), 0) % rows
        slot = dot(spread, table.astype(BF16)).astype(jnp.int32)
        low = slot == place
        high = (slot >= 0) & (slot + capacity == place)
        pick[0] = low.astype(F32).astype(BF16)
        pick[1] = high.astype(F32).astype(BF16)
        expert = iota((experts, tokens), 0)
        gates = gates_ref[...]
        weight = jnp.where(expert == ids[0:1, :], gates[0:1, :], gates[1:2, :])
        coarse = weight.astype(BF16)
        fine = (weight - coarse.astype(F32)).astype(BF16)
        for part, value in enumerate((coarse, fine)):
            wide = dot(spread, value)
            for half, chosen in enumerate((low, high)):
                mix_ref[half, part] = jnp.where(chosen, wide, 0.0).T.astype(BF16)
        whose = iota((count, tokens), 0) // rows
        for choice in range(2):
            own_ref[choice] = (low & (whose == ids[choice : choice + 1, :])).astype(F32).astype(BF16)

    count = experts * rows
    width = send_ref.shape[2]
    for part, (left, right) in enumerate(((tl, th), (gl, gh))):
        moved = dot(pick[0], left[...]) + dot(pick[1], right[...])
        send_ref[:, part * rows : (part + 1) * rows, :] = moved.astype(BF16).reshape(experts, rows, width)


def dispatch(ids, gates, tokens, grads, experts, capacity):
    count, width = tokens.shape
    rows = 2 * capacity
    blocks, block = 4, width // 8
    low = pl.BlockSpec((count, block), lambda i: (0, i))
    high = pl.BlockSpec((count, block), lambda i: (0, i + blocks))
    whole = lambda shape: pl.BlockSpec(shape, lambda i: (0,) * len(shape))
    return pl.pallas_call(
        functools.partial(dispatch_kernel, experts, capacity),
        grid=(blocks,),
        in_specs=[whole(ids.shape), whole(gates.shape), low, high, low, high],
        out_specs=[
            pl.BlockSpec((experts, 2 * rows, block), lambda i: (0, 0, i)),
            whole((2, 2, count, experts * rows)),
            whole((2, experts * rows, count)),
        ],
        out_shape=[
            jax.ShapeDtypeStruct((experts, 2 * rows, width // 2), BF16),
            jax.ShapeDtypeStruct((2, 2, count, experts * rows), BF16),
            jax.ShapeDtypeStruct((2, experts * rows, count), BF16),
        ],
        scratch_shapes=[pltpu.VMEM((2, experts * rows, count), BF16)],
        compiler_params=params("arbitrary"),
        name="dispatch",
    )(ids, gates, tokens, tokens, grads, grads)


def unpack_kernel(capacity, recv_ref, tokens_ref, grads_ref):
    slots = tokens_ref.shape[0]
    total = recv_ref.shape[0]
    row, column = iota((slots, total), 0), iota((slots, total), 1)
    base = (row // capacity) * (4 * capacity) + row % capacity
    half = pl.program_id(0) % 2
    for part, out in enumerate((tokens_ref, grads_ref)):
        take = column == base + (2 * part + half) * capacity
        out[...] = dot(take.astype(F32).astype(BF16), recv_ref[...]).astype(BF16)


def unpack(recv, capacity):
    total, half_width = recv.shape
    slots = total // 4
    blocks = 2
    block = half_width // blocks
    out = pl.BlockSpec((slots, block), lambda i: (0, (i % 2) * blocks + i // 2))
    return pl.pallas_call(
        functools.partial(unpack_kernel, capacity),
        grid=(2 * blocks,),
        in_specs=[pl.BlockSpec((total, block), lambda i: (0, i // 2))],
        out_specs=[out, out],
        out_shape=[jax.ShapeDtypeStruct((slots, 2 * half_width), BF16)] * 2,
        compiler_params=params("arbitrary"),
        name="unpack",
    )(recv)


def expert_kernel(capacity, blocks, x_ref, g_ref, w_ref, out_ref, up, hidden, active_grad):
    step = pl.program_id(0)
    slots, hidden_width = hidden.shape
    part_hidden = dot(x_ref[...], w_ref[:, :hidden_width])
    part_grad = dot(g_ref[...], w_ref[:, hidden_width:])
    up[step] = w_ref[:, :hidden_width]

    @pl.when(step == 0)
    def _():
        hidden[...] = part_hidden
        active_grad[...] = part_grad

    @pl.when(step > 0)
    def _():
        hidden[...] += part_hidden
        active_grad[...] += part_grad

    @pl.when(step == blocks - 1)
    def _():
        h = hidden[...]
        a = active_grad[...]
        cdf = 0.5 * (1.0 + lax.erf(h * 0.7071067811865476))
        density = jnp.exp(-0.5 * h * h) * 0.3989422804014327
        active = (h * cdf).astype(BF16).astype(F32)
        gate = jnp.sum(active * a, axis=1, keepdims=True).astype(BF16)
        hidden_grad = (a * (cdf + h * density)).astype(BF16)
        rows = 2 * capacity
        total = 2 * slots
        row, column = iota((total, slots), 0), iota((total, slots), 1)
        base = (row // rows) * capacity + row % rows
        low = (column == base) & (row % rows < capacity)
        high = (column == base - capacity) & (row % rows >= capacity)
        low, high = low.astype(F32).astype(BF16), high.astype(F32).astype(BF16)
        block = up.shape[1]
        for i in range(blocks // 2):
            left = dot_t(hidden_grad, up[i]).astype(BF16)
            right = dot_t(hidden_grad, up[i + blocks // 2]).astype(BF16)
            out_ref[:, i * block : (i + 1) * block] = (dot(low, left) + dot(high, right)).astype(BF16)
        lanes = jnp.broadcast_to(gate, (slots, 128))
        out_ref[:, blocks // 2 * block :] = dot(low, lanes).astype(BF16)


def expert(x, g, weights, capacity):
    slots, width = x.shape
    wide = weights.shape[1]
    blocks = 8
    block = width // blocks
    columns = pl.BlockSpec((slots, block), lambda i: (0, i))
    return pl.pallas_call(
        functools.partial(expert_kernel, capacity, blocks),
        grid=(blocks,),
        in_specs=[columns, columns, pl.BlockSpec((block, wide), lambda i: (i, 0))],
        out_specs=pl.BlockSpec((2 * slots, width // 2 + 128), lambda i: (0, 0)),
        out_shape=jax.ShapeDtypeStruct((2 * slots, width // 2 + 128), BF16),
        scratch_shapes=[
            pltpu.VMEM((blocks, block, wide // 2), BF16),
            pltpu.VMEM((slots, wide // 2), F32),
            pltpu.VMEM((slots, wide // 2), F32),
        ],
        compiler_params=params("arbitrary"),
        name="expert",
    )(x, g, weights)


def combine_kernel(back_ref, gate_ref, mix_ref, own_ref, tokens_ref, gates_ref):
    half = pl.program_id(0) % 2
    total = dot(mix_ref[half, 0], back_ref[...]) + dot(mix_ref[half, 1], back_ref[...])
    tokens_ref[...] = total.astype(BF16)

    @pl.when(pl.program_id(0) == 0)
    def _():
        column = gate_ref[:, 0:1].astype(F32)
        for choice in range(2):
            picked = jnp.sum(own_ref[choice].astype(F32) * column, axis=0, keepdims=True)
            gates_ref[choice : choice + 1, :] = picked.astype(BF16)


def combine(back, mix, own):
    total, wide = back.shape
    count = mix.shape[2]
    half_width = wide - 128
    blocks = 4
    block = half_width // blocks
    whole = lambda shape: pl.BlockSpec(shape, lambda i: (0,) * len(shape))
    return pl.pallas_call(
        combine_kernel,
        grid=(2 * blocks,),
        in_specs=[
            pl.BlockSpec((total, block), lambda i: (0, i // 2)),
            pl.BlockSpec((total, 128), lambda i: (0, half_width // 128)),
            whole(mix.shape),
            whole(own.shape),
        ],
        out_specs=[
            pl.BlockSpec((count, block), lambda i: (0, (i % 2) * blocks + i // 2)),
            whole((2, count)),
        ],
        out_shape=[
            jax.ShapeDtypeStruct((count, 2 * half_width), BF16),
            jax.ShapeDtypeStruct((2, count), BF16),
        ],
        compiler_params=params("arbitrary"),
        name="combine",
    )(back, back, mix, own)


def body(tokens, expert_ids, gate_probs, up_weight, down_weight, out_grad):
    experts = lax.axis_size("expert")
    count, width = tokens.shape
    capacity = 3 * count // (2 * experts)
    shard = jnp.concatenate([up_weight[0], down_weight[0].T], axis=1)
    weights = lax.all_gather(shard, "fsdp", axis=0, tiled=True)
    send, mix, own = dispatch(expert_ids.T, gate_probs.T, tokens, out_grad, experts, capacity)
    recv = lax.all_to_all(send, "expert", split_axis=0, concat_axis=0, tiled=True)
    x, g = unpack(recv.reshape(4 * experts * capacity, width // 2), capacity)
    packed = expert(x, g, weights, capacity)
    back = lax.all_to_all(
        packed.reshape(experts, 2 * capacity, width // 2 + 128),
        "expert",
        split_axis=0,
        concat_axis=0,
        tiled=True,
    )
    d_tokens, d_gates = combine(back.reshape(packed.shape), mix, own)
    return d_tokens, d_gates.T


def solution(mesh):
    placed = (
        P(("fsdp", "expert"), None),
        P(("fsdp", "expert"), None),
        P(("fsdp", "expert"), None),
        P("expert", "fsdp", None),
        P("expert", None, "fsdp"),
        P(("fsdp", "expert"), None),
    )
    return jax.shard_map(
        body,
        mesh=mesh,
        in_specs=placed,
        out_specs=(P(("fsdp", "expert"), None), P(("fsdp", "expert"), None)),
        check_vma=False,
    )
```

time: 260 us -> 161 us (0.62)
  waiting for transfers between devices: 163 us -> 38.8 us
  blocking collectives: 0 us -> 72.2 us
  Pallas kernels: 0 us -> 33 us
  starting transfers between devices: 27.6 us -> 0.04 us
  local copies, waits for them, and re-layouts: 26.7 us -> 1.06 us
  matrix products: 19.1 us -> 0 us
  other arithmetic: 6.7 us -> 1.7 us
    all_to_all x0 -> x2, blocking collectives: none -> 72.2 us  [the longest x1 42.8 us: body(): lax.all_to_all(send, 'expert', split_axis=0, concat_axis=0, tiled=True)]
    all_to_all x4 -> x0, waiting for transfers between devices: 66.4 us -> none  [the longest x1 23.8 us: body(): lax.all_to_all(send_grads, 'expert', split_axis=0, concat_axis=0, tiled=T...]
    all_gather x2 -> x1, waiting for transfers between devices: 95.5 us -> 38.8 us  [body(): weights = lax.all_gather(shard, 'fsdp', axis=0, tiled=True)]
    pallas_call x0 -> x4, Pallas kernels: none -> 33 us  [the longest x1 14.2 us: expert(): pl.pallas_call(functools.partial(expert_kernel, capacity, blocks), grid=(...]
    all_to_all x4 -> x0, starting transfers between devices: 27.5 us -> none  [the longest x1 7.58 us: body(): lax.all_to_all(send_tokens, 'expert', split_axis=0, concat_axis=0, tiled=...]
    dot_general x5 -> x0, matrix products: 19.1 us -> none  [the longest x2 11 us: right_product(): lax.dot_general(left, right, (((1,), (1,)), ((), ())), preferred_element_...]
    reshape x7 -> x0, local copies, waits for them, and re-layouts: 12.9 us -> none  [the longest x1 3.39 us: body(): send_grads = jnp.dot(match_rows, out_grad, preferred_element_type=jnp.flo...]
    convert_element_type x2 -> x0, local copies, waits for them, and re-layouts: 6.13 us -> none  [the longest x1 5.44 us: body(): picked.astype(jnp.float32) * weight[:, None]]
  transfers between devices with their start and end apart: 6 -> 1, of which waited for: 5 -> 1; matrix products, arithmetic and copies ran while one was open for 11% -> 0% of each run, Pallas kernels for 0% -> 8%
where the time goes in v1:
time: 161 us
  blocking collectives  72.2 us (45%)
  waiting for transfers between devices  38.8 us (24%)
  Pallas kernels  33 us (20%)
  between operations  14 us (9%)
  other arithmetic  1.7 us (1%)
    all_to_all x1, blocking collectives, body(): lax.all_to_all(send, 'expert', split_axis=0, concat_axis=0, tiled=True)  42.8 us
    all_gather x1, waiting for transfers between devices, body(): weights = lax.all_gather(shard, 'fsdp', axis=0, tiled=True)  38.8 us
    all_to_all x1, blocking collectives, body(): lax.all_to_all(packed.reshape(experts, 2 * capacity, width // 2 + 128), '...  29.4 us
    pallas_call x1, Pallas kernels, expert(): pl.pallas_call(functools.partial(expert_kernel, capacity, blocks), grid=(...  14.2 us
    pallas_call x1, Pallas kernels, combine(): pl.pallas_call(combine_kernel, grid=(2 * blocks,), in_specs=[pl.BlockSpec...  6.72 us
    pallas_call x1, Pallas kernels, unpack(): pl.pallas_call(functools.partial(unpack_kernel, capacity), grid=(2 * bloc...  6.34 us
    pallas_call x1, Pallas kernels, dispatch(): pl.pallas_call(functools.partial(dispatch_kernel, experts, capacity), gri...  5.75 us
  transfers between devices with their start and end apart: 1, of which 1 were waited for; matrix products, arithmetic and copies ran while one was open for 0% of the time, Pallas kernels for 8%

profile of v1, /device:TPU:1, one launch (start us, length us, event | category | flops | bytes accessed | tf_op | source)
XLA Modules:
  0.0 160.9 jit_solution(9521957735608448860)
XLA Ops:
  7.2 0.0 all-gather.2.cloned.1.call-start
  7.2 1.1 copy.8
  8.3 1.7 %pad_maximum_fusion = bf16[128,1536]{1,0:T(8,128)(2,1)} fusion(bf16[128,768]{1,0:T(8,128)(2,1)S(1)} %bitcast.14, bf16[128,768]{1,0:T(8,128)(2,1)} %bitcast.15), kind=kLoop, calls=%fused_computation | loop fusion | flops 786432 | bytes 786432 | tf_op jit(solution)/shard_map/concatenate | solution.py:240
  10.0 0.0 all-gather.2.cloned.1.call-update
  10.0 5.7 %dispatch.1 = (bf16[16,48,2048]{2,1,0:T(8,128)(2,1)}, bf16[2,2,128,384]{3,2,1,0:T(8,128)(2,1)}, bf16[2,384,128]{2,1,0:T(8,128)(2,1)}) custom-call(s32[2,128]{1,0:T(2,128)} %bitcast.16, f32[2,128]{1,0:T(2,128)} %bitcast.17, bf16[128,4096]{1,0:T(8,128)(2,1)} %th.1, bf16[128,4096]{1,0:T(8,128)(2,1)} %th.1, bf16[128,4096]{1,0:T(8,128)(2,1)} %gh.1, ...), custom_call_target="tpu_custom_call" | custom-call | tf_op jit(solution)/shard_map/dispatch/pallas_call | solution.py:82
  15.7 42.8 %all_to_all.10 = bf16[16,48,2048]{2,1,0:T(8,128)(2,1)} all-to-all(bf16[16,48,2048]{2,1,0:T(8,128)(2,1)} %get-tuple-element.9), channel_id=1, replica_groups=mesh['fsdp'=32,'expert'=16] {'expert'}, dimensions={0} | all-to-all | bytes 6291456 | tf_op jit(solution)/shard_map/all_to_all | solution.py:243
  58.6 6.3 %unpack.1 = (bf16[192,4096]{1,0:T(8,128)(2,1)}, bf16[192,4096]{1,0:T(8,128)(2,1)}) custom-call(bf16[768,2048]{1,0:T(8,128)(2,1)} %bitcast.12), custom_call_target="tpu_custom_call" | custom-call | tf_op jit(solution)/shard_map/unpack/pallas_call | solution.py:119
  64.9 38.8 %all-gather.2.cloned.1.call-done.w_ref = bf16[4096,1536]{1,0:T(8,128)(2,1)} async-done(((bf16[128,1536]{1,0:T(8,128)(2,1)}), bf16[4096,1536]{1,0:T(8,128)(2,1)}) %all-gather.2.cloned.1.call-update) | async-done | bytes 12582928 | tf_op jit(solution)/shard_map/all_gather | solution.py:241
  103.7 14.2 %expert.1 = bf16[384,2176]{1,0:T(8,128)(2,1)} custom-call(bf16[192,4096]{1,0:T(8,128)(2,1)} %get-tuple-element.10.x_ref, bf16[192,4096]{1,0:T(8,128)(2,1)} %get-tuple-element.11.g_ref, bf16[4096,1536]{1,0:T(8,128)(2,1)} %all-gather.2.cloned.1.call-done.w_ref), custom_call_target="tpu_custom_call" | custom-call | tf_op jit(solution)/shard_map/expert/pallas_call | solution.py:178
  117.9 29.4 %all_to_all.11 = bf16[16,24,2176]{2,1,0:T(8,128)(2,1)} all-to-all(bf16[16,24,2176]{2,1,0:T(8,128)(2,1)} %bitcast.13), channel_id=1, replica_groups=mesh['fsdp'=32,'expert'=16] {'expert'}, dimensions={0} | all-to-all | bytes 3342336 | tf_op jit(solution)/shard_map/all_to_all | solution.py:246
  147.3 6.7 %combine.1 = (bf16[128,4096]{1,0:T(8,128)(2,1)}, bf16[2,128]{1,0:T(2,128)(2,1)}) custom-call(bf16[384,2176]{1,0:T(8,128)(2,1)} %bitcast.10, bf16[384,2176]{1,0:T(8,128)(2,1)} %bitcast.11, bf16[2,2,128,384]{3,2,1,0:T(8,128)(2,1)} %get-tuple-element.12.mix_ref, bf16[2,384,128]{2,1,0:T(8,128)(2,1)} %get-tuple-element.13.own_ref), custom_call_target="tpu_custom_call" | custom-call | tf_op jit(solution)/shard_map/combine/pallas_call | solution.py:214
Async XLA Ops:
  7.2 96.6 %all-gather.2.cloned.1.call-start = ((), (), s32[]{:S(2)}) async-start(), calls=%async_computation.2 | async-start | bytes 12976128 | tf_op jit(solution)/shard_map/all_gather | solution.py:241
Sparse Core Ops, SparseCore 0:
  10.7 92.9 all-gather.1

commit v2 on v1

v2 whole, which is shorter than its diff:
```python
import functools

import jax
import jax.numpy as jnp
from jax import lax
from jax.experimental import pallas as pl
from jax.experimental.pallas import tpu as pltpu
from jax.sharding import PartitionSpec as P

F32, BF16 = jnp.float32, jnp.bfloat16
VMEM_LIMIT = 56 * 1024 * 1024


def dot(left, right):
    return jnp.dot(left, right, preferred_element_type=F32)


def dot_t(left, right):
    return lax.dot_general(left, right, (((1,), (1,)), ((), ())), preferred_element_type=F32)


def iota(shape, axis):
    return lax.broadcasted_iota(jnp.int32, shape, axis)


def params(*semantics):
    return pltpu.CompilerParams(dimension_semantics=semantics, vmem_limit_bytes=VMEM_LIMIT)


def slot_table(ids, experts, capacity):
    tokens = ids.shape[1]
    expert = iota((experts, tokens), 0)
    named = (expert == ids[0:1, :]) | (expert == ids[1:2, :])
    before = (iota((tokens, tokens), 0) < iota((tokens, tokens), 1)).astype(F32).astype(BF16)
    count = dot(named.astype(F32).astype(BF16), before)
    return jnp.where(named & (count < capacity), count, -1.0)


def dispatch_kernel(experts, capacity, ids_ref, gates_ref, tl, th, gl, gh, send_ref, mix_ref, own_ref, pick):
    rows = 2 * capacity
    tokens = ids_ref.shape[1]

    @pl.when(pl.program_id(0) == 0)
    def _():
        ids = ids_ref[...]
        table = slot_table(ids, experts, capacity)
        count = experts * rows
        spread = (iota((count, experts), 0) // rows == iota((count, experts), 1)).astype(F32).astype(BF16)
        place = iota((count, tokens), 0) % rows
        slot = dot(spread, table.astype(BF16)).astype(jnp.int32)
        low = slot == place
        high = (slot >= 0) & (slot + capacity == place)
        pick[0] = low.astype(F32).astype(BF16)
        pick[1] = high.astype(F32).astype(BF16)
        expert = iota((experts, tokens), 0)
        gates = gates_ref[...]
        weight = jnp.where(expert == ids[0:1, :], gates[0:1, :], gates[1:2, :])
        coarse = weight.astype(BF16)
        fine = (weight - coarse.astype(F32)).astype(BF16)
        for part, value in enumerate((coarse, fine)):
            wide = dot(spread, value)
            for half, chosen in enumerate((low, high)):
                mix_ref[half, part] = jnp.where(chosen, wide, 0.0).T.astype(BF16)
        whose = iota((count, tokens), 0) // rows
        for choice in range(2):
            own_ref[choice] = (low & (whose == ids[choice : choice + 1, :])).astype(F32).astype(BF16)

    count = experts * rows
    width = send_ref.shape[2]
    for part, (left, right) in enumerate(((tl, th), (gl, gh))):
        moved = dot(pick[0], left[...]) + dot(pick[1], right[...])
        send_ref[:, part * rows : (part + 1) * rows, :] = moved.astype(BF16).reshape(experts, rows, width)


def dispatch(ids, gates, tokens, grads, experts, capacity):
    count, width = tokens.shape
    rows = 2 * capacity
    blocks, block = 4, width // 8
    low = pl.BlockSpec((count, block), lambda i: (0, i))
    high = pl.BlockSpec((count, block), lambda i: (0, i + blocks))
    whole = lambda shape: pl.BlockSpec(shape, lambda i: (0,) * len(shape))
    return pl.pallas_call(
        functools.partial(dispatch_kernel, experts, capacity),
        grid=(blocks,),
        in_specs=[whole(ids.shape), whole(gates.shape), low, high, low, high],
        out_specs=[
            pl.BlockSpec((experts, 2 * rows, block), lambda i: (0, 0, i)),
            whole((2, 2, count, experts * rows)),
            whole((2, experts * rows, count)),
        ],
        out_shape=[
            jax.ShapeDtypeStruct((experts, 2 * rows, width // 2), BF16),
            jax.ShapeDtypeStruct((2, 2, count, experts * rows), BF16),
            jax.ShapeDtypeStruct((2, experts * rows, count), BF16),
        ],
        scratch_shapes=[pltpu.VMEM((2, experts * rows, count), BF16)],
        compiler_params=params("arbitrary"),
        name="dispatch",
    )(ids, gates, tokens, tokens, grads, grads)


IN_VMEM = pl.BlockSpec(memory_space=pltpu.VMEM)
IN_HBM = pl.BlockSpec(memory_space=pltpu.HBM)


def unpack_kernel(capacity, recv_ref, tokens_ref, grads_ref):
    slots, width = tokens_ref.shape
    total, half = recv_ref.shape
    row, column = iota((slots, total), 0), iota((slots, total), 1)
    base = (row // capacity) * (4 * capacity) + row % capacity
    block = half // 4
    for part, out in enumerate((tokens_ref, grads_ref)):
        for side in range(2):
            take = (column == base + (2 * part + side) * capacity).astype(F32).astype(BF16)
            for i in range(4):
                start = side * half + i * block
                moved = dot(take, recv_ref[:, i * block : (i + 1) * block])
                out[:, start : start + block] = moved.astype(BF16)


def unpack(recv, capacity):
    total, half = recv.shape
    return pl.pallas_call(
        functools.partial(unpack_kernel, capacity),
        in_specs=[IN_VMEM],
        out_specs=[IN_VMEM, IN_VMEM],
        out_shape=[jax.ShapeDtypeStruct((total // 4, 2 * half), BF16)] * 2,
        compiler_params=pltpu.CompilerParams(vmem_limit_bytes=16 * 1024 * 1024),
        name="unpack",
    )(recv)


def expert_kernel(capacity, cuts, x_ref, g_ref, w_hbm, out_ref, w, arrived):
    slots, width = x_ref.shape
    wide = w.shape[1] // 2
    loads = []
    for i in range(len(cuts) - 1):
        part = pl.ds(cuts[i], cuts[i + 1] - cuts[i])
        loads.append(pltpu.make_async_copy(w_hbm.at[part], w.at[part], arrived.at[i]))
        loads[i].start()
    rows = 2 * capacity
    row, column = iota((2 * slots, slots), 0), iota((2 * slots, slots), 1)
    base = (row // rows) * capacity + row % rows
    low = (column == base) & (row % rows < capacity)
    high = (column == base - capacity) & (row % rows >= capacity)
    low, high = low.astype(F32).astype(BF16), high.astype(F32).astype(BF16)
    h = a = None
    for i in range(len(cuts) - 1):
        loads[i].wait()
        part = slice(cuts[i], cuts[i + 1])
        more_h, more_a = dot(x_ref[:, part], w[part, :wide]), dot(g_ref[:, part], w[part, wide:])
        h, a = (more_h, more_a) if h is None else (h + more_h, a + more_a)
    cdf = 0.5 * (1.0 + lax.erf(h * 0.7071067811865476))
    density = jnp.exp(-0.5 * h * h) * 0.3989422804014327
    active = (h * cdf).astype(BF16).astype(F32)
    gate = jnp.sum(active * a, axis=1, keepdims=True).astype(BF16)
    hidden_grad = (a * (cdf + h * density)).astype(BF16)
    half = width // 2
    block = half // 4
    for i in range(4):
        left = dot_t(hidden_grad, w[i * block : (i + 1) * block, :wide]).astype(BF16)
        right = dot_t(hidden_grad, w[half + i * block : half + (i + 1) * block, :wide]).astype(BF16)
        out_ref[:, i * block : (i + 1) * block] = (dot(low, left) + dot(high, right)).astype(BF16)
    out_ref[:, half:] = dot(low, jnp.broadcast_to(gate, (slots, 128))).astype(BF16)


def expert(x, g, weights, capacity):
    slots, width = x.shape
    cuts = tuple(width * eighth // 8 for eighth in (0, 1, 2, 4, 6, 8))
    return pl.pallas_call(
        functools.partial(expert_kernel, capacity, cuts),
        in_specs=[IN_VMEM, IN_VMEM, IN_HBM],
        out_specs=IN_VMEM,
        out_shape=jax.ShapeDtypeStruct((2 * slots, width // 2 + 128), BF16),
        scratch_shapes=[
            pltpu.VMEM(weights.shape, BF16),
            pltpu.SemaphoreType.DMA((len(cuts) - 1,)),
        ],
        compiler_params=pltpu.CompilerParams(vmem_limit_bytes=40 * 1024 * 1024),
        name="expert",
    )(x, g, weights)


def combine_kernel(blocks, back_ref, mix_ref, own_ref, tokens_hbm, gates_ref, out, left):
    count, width = out.shape
    half = width // 2
    block = half // blocks
    stores = []
    for i in range(blocks):
        total = dot(mix_ref[...], back_ref[:, i * block : (i + 1) * block])
        for side in range(2):
            coarse, fine = (total[(2 * side + j) * count : (2 * side + j + 1) * count] for j in range(2))
            start = side * half + i * block
            out[:, start : start + block] = (coarse + fine).astype(BF16)
            part = pl.ds(start, block)
            stores.append(pltpu.make_async_copy(out.at[:, part], tokens_hbm.at[:, part], left.at[2 * i + side]))
            stores[-1].start()
    column = back_ref[:, half : half + 1].astype(F32)
    for choice in range(2):
        picked = jnp.sum(own_ref[choice].astype(F32) * column, axis=0, keepdims=True)
        gates_ref[choice : choice + 1, :] = picked.astype(BF16)
    for store in stores:
        store.wait()


def combine(back, mix, own):
    half = back.shape[1] - 128
    count = own.shape[2]
    blocks = 4
    return pl.pallas_call(
        functools.partial(combine_kernel, blocks),
        in_specs=[IN_VMEM, IN_VMEM, IN_VMEM],
        out_specs=[IN_HBM, IN_VMEM],
        out_shape=[
            jax.ShapeDtypeStruct((count, 2 * half), BF16),
            jax.ShapeDtypeStruct((2, count), BF16),
        ],
        scratch_shapes=[
            pltpu.VMEM((count, 2 * half), BF16),
            pltpu.SemaphoreType.DMA((2 * blocks,)),
        ],
        compiler_params=pltpu.CompilerParams(vmem_limit_bytes=16 * 1024 * 1024),
        name="combine",
    )(back, mix, own)


def join_kernel(up_ref, down_ref, out_ref):
    width = up_ref.shape[2]
    out_ref[:, :width] = up_ref[0]
    out_ref[:, width:] = down_ref[0].T


def join(up, down):
    return pl.pallas_call(
        join_kernel,
        in_specs=[IN_VMEM, IN_VMEM],
        out_specs=IN_VMEM,
        out_shape=jax.ShapeDtypeStruct((up.shape[1], 2 * up.shape[2]), BF16),
        name="join",
    )(up, down)


def body(tokens, expert_ids, gate_probs, up_weight, down_weight, out_grad):
    experts = lax.axis_size("expert")
    count, width = tokens.shape
    capacity = 3 * count // (2 * experts)
    weights = lax.all_gather(join(up_weight, down_weight), "fsdp", axis=0, tiled=True)
    send, mix, own = dispatch(expert_ids.T, gate_probs.T, tokens, out_grad, experts, capacity)
    recv = lax.all_to_all(send, "expert", split_axis=0, concat_axis=0, tiled=True)
    x, g = unpack(recv.reshape(4 * experts * capacity, width // 2), capacity)
    packed = expert(x, g, weights, capacity)
    back = lax.all_to_all(
        packed.reshape(experts, 2 * capacity, width // 2 + 128),
        "expert",
        split_axis=0,
        concat_axis=0,
        tiled=True,
    )
    d_tokens, d_gates = combine(back.reshape(packed.shape), mix.reshape(4 * count, -1), own)
    return d_tokens, d_gates.T


def solution(mesh):
    placed = (
        P(("fsdp", "expert"), None),
        P(("fsdp", "expert"), None),
        P(("fsdp", "expert"), None),
        P("expert", "fsdp", None),
        P("expert", None, "fsdp"),
        P(("fsdp", "expert"), None),
    )
    return jax.shard_map(
        body,
        mesh=mesh,
        in_specs=placed,
        out_specs=(P(("fsdp", "expert"), None), P(("fsdp", "expert"), None)),
        check_vma=False,
    )
```

time: 161 us -> 151 us (0.938)
  Pallas kernels: 33 us -> 21.6 us
  waiting for transfers between devices: 38.8 us -> 42.5 us
  other arithmetic: 1.7 us -> 0 us
    pallas_call x3 -> x4, Pallas kernels: 27.3 us -> 15.9 us  [the longest x1 8.87 us: expert(): pl.pallas_call(functools.partial(expert_kernel, capacity, cuts), in_specs...]
    all_gather x1, waiting for transfers between devices: 38.8 us -> 42.5 us  [body(): lax.all_gather(join(up_weight, down_weight), 'fsdp', axis=0, tiled=True)]
    concatenate x1 -> x0, other arithmetic: 1.7 us -> none  [body(): shard = jnp.concatenate([up_weight[0], down_weight[0].T], axis=1)]
  transfers between devices with their start and end apart: 1 -> 1, of which waited for: 1 -> 1; matrix products, arithmetic and copies ran while one was open for 0% -> 0% of each run, Pallas kernels for 8% -> 6%
where the time goes in v2:
time: 151 us
  blocking collectives  72.6 us (48%)
  waiting for transfers between devices  42.5 us (28%)
  Pallas kernels  21.6 us (14%)
  between operations  14.1 us (9%)
    all_to_all x1, blocking collectives, body(): lax.all_to_all(send, 'expert', split_axis=0, concat_axis=0, tiled=True)  43 us
    all_gather x1, waiting for transfers between devices, body(): lax.all_gather(join(up_weight, down_weight), 'fsdp', axis=0, tiled=True)  42.5 us
    all_to_all x1, blocking collectives, body(): lax.all_to_all(packed.reshape(experts, 2 * capacity, width // 2 + 128), '...  29.6 us
    pallas_call x1, Pallas kernels, expert(): pl.pallas_call(functools.partial(expert_kernel, capacity, cuts), in_specs...  8.87 us
    pallas_call x1, Pallas kernels, dispatch(): pl.pallas_call(functools.partial(dispatch_kernel, experts, capacity), gri...  5.74 us
  transfers between devices with their start and end apart: 1, of which 1 were waited for; matrix products, arithmetic and copies ran while one was open for 0% of the time, Pallas kernels for 6%

profile of v2, /device:TPU:1, one launch (start us, length us, event | category | flops | bytes accessed | tf_op | source)
XLA Modules:
  0.0 150.8 jit_solution(3951590135097988642)
XLA Ops:
  7.2 0.0 all-gather.2.cloned.1.call-start
  7.2 1.9 %join.1 = bf16[128,1536]{1,0:T(8,128)(2,1)} custom-call(bf16[1,128,768]{2,1,0:T(8,128)(2,1)} %up_ref.1, bf16[1,768,128]{2,1,0:T(8,128)(2,1)} %down_ref.1), custom_call_target="tpu_custom_call" | custom-call | tf_op jit(solution)/shard_map/join/pallas_call | solution.py:234
  9.1 0.0 all-gather.2.cloned.1.call-update
  9.1 5.7 %dispatch.1 = (bf16[16,48,2048]{2,1,0:T(8,128)(2,1)}, bf16[2,2,128,384]{3,2,1,0:T(8,128)(2,1)}, bf16[2,384,128]{2,1,0:T(8,128)(2,1)}) custom-call(s32[2,128]{1,0:T(2,128)} %bitcast.11, f32[2,128]{1,0:T(2,128)} %bitcast.12, bf16[128,4096]{1,0:T(8,128)(2,1)} %th.1, bf16[128,4096]{1,0:T(8,128)(2,1)} %th.1, bf16[128,4096]{1,0:T(8,128)(2,1)} %gh.1, ...), custom_call_target="tpu_custom_call" | custom-call | tf_op jit(solution)/shard_map/dispatch/pallas_call | solution.py:82
  14.8 43.0 %all_to_all.10 = bf16[16,48,2048]{2,1,0:T(8,128)(2,1)S(1)} all-to-all(bf16[16,48,2048]{2,1,0:T(8,128)(2,1)} %get-tuple-element.9), channel_id=1, replica_groups=mesh['fsdp'=32,'expert'=16] {'expert'}, dimensions={0} | all-to-all | bytes 6291456 | tf_op jit(solution)/shard_map/all_to_all | solution.py:249
  57.9 2.6 %unpack.1 = (bf16[192,4096]{1,0:T(8,128)(2,1)S(1)}, bf16[192,4096]{1,0:T(8,128)(2,1)S(1)}) custom-call(bf16[768,2048]{1,0:T(8,128)(2,1)S(1)} %bitcast.7), custom_call_target="tpu_custom_call" | custom-call | tf_op jit(solution)/shard_map/unpack/pallas_call | solution.py:123
  60.5 42.5 %all-gather.2.cloned.1.call-done.w_hbm = bf16[4096,1536]{1,0:T(8,128)(2,1)} async-done(((bf16[128,1536]{1,0:T(8,128)(2,1)}), bf16[4096,1536]{1,0:T(8,128)(2,1)}) %all-gather.2.cloned.1.call-update) | async-done | bytes 12582928 | tf_op jit(solution)/shard_map/all_gather | solution.py:247
  103.0 8.9 %expert.1 = bf16[384,2176]{1,0:T(8,128)(2,1)S(1)} custom-call(bf16[192,4096]{1,0:T(8,128)(2,1)S(1)} %get-tuple-element.10.x_ref, bf16[192,4096]{1,0:T(8,128)(2,1)S(1)} %get-tuple-element.11.g_ref, bf16[4096,1536]{1,0:T(8,128)(2,1)} %all-gather.2.cloned.1.call-done.w_hbm), custom_call_target="tpu_custom_call" | custom-call | tf_op jit(solution)/shard_map/expert/pallas_call | solution.py:170
  111.8 0.0 copy-start
  111.8 0.0 copy-start.1
  111.9 29.6 %all_to_all.11 = bf16[16,24,2176]{2,1,0:T(8,128)(2,1)S(1)} all-to-all(bf16[16,24,2176]{2,1,0:T(8,128)(2,1)S(1)} %bitcast.8), channel_id=1, replica_groups=mesh['fsdp'=32,'expert'=16] {'expert'}, dimensions={0} | all-to-all | bytes 3342336 | tf_op jit(solution)/shard_map/all_to_all | solution.py:252
  141.5 0.0 copy-done
  141.5 0.0 copy-done.1
  141.5 2.5 %combine.1 = (bf16[128,4096]{1,0:T(8,128)(2,1)}, bf16[2,128]{1,0:T(2,128)(2,1)}) custom-call(bf16[384,2176]{1,0:T(8,128)(2,1)S(1)} %bitcast.9, bf16[512,384]{1,0:T(8,128)(2,1)S(1)} %bitcast.10, bf16[2,384,128]{2,1,0:T(8,128)(2,1)S(1)} %copy-done.1), custom_call_target="tpu_custom_call" | custom-call | tf_op jit(solution)/shard_map/combine/pallas_call | solution.py:210
Async XLA Ops:
  7.2 95.8 %all-gather.2.cloned.1.call-start = ((), (), s32[]{:S(2)}) async-start(), calls=%async_computation.2 | async-start | bytes 12976128 | tf_op jit(solution)/shard_map/all_gather | solution.py:247
  111.8 29.6 %copy-start = (bf16[2,2,128,384]{3,2,1,0:T(8,128)(2,1)S(1)}, bf16[2,2,128,384]{3,2,1,0:T(8,128)(2,1)}, u32[]{:S(2)}) copy-start(bf16[2,2,128,384]{3,2,1,0:T(8,128)(2,1)} %get-tuple-element.12) | copy-start | bytes 1179652
  111.8 29.6 %copy-start.1 = (bf16[2,384,128]{2,1,0:T(8,128)(2,1)S(1)}, bf16[2,384,128]{2,1,0:T(8,128)(2,1)}, u32[]{:S(2)}) copy-start(bf16[2,384,128]{2,1,0:T(8,128)(2,1)} %get-tuple-element.13.own_ref) | copy-start | bytes 589828
Sparse Core Ops, SparseCore 0:
  10.1 92.7 all-gather.1

commit v3 on v2

--- a/solution.py
+++ b/solution.py
@@ -1,4 +1,5 @@
 import functools
+import math
 
 import jax
 import jax.numpy as jnp
@@ -240,22 +241,40 @@
     )(up, down)
 
 
+def exchange_orders(side):
+    first = [((i % side + i // side) % side) * side + i % side for i in range(side * side)]
+    return first, [(device % side) * side + device // side for device in first]
+
+
+def place_in_order(ids, side, core):
+    x, y = ids // side, ids % side
+    along, across = jnp.where(core == 0, x, y), jnp.where(core == 0, y, x)
+    return ((along - across) % side) * side + across
+
+
 def body(tokens, expert_ids, gate_probs, up_weight, down_weight, out_grad):
     experts = lax.axis_size("expert")
+    planes = lax.axis_size("fsdp")
+    side = math.isqrt(experts)
+    orders = exchange_orders(side)
+    groups = [[plane * experts + device for device in orders[plane % 2]] for plane in range(planes)]
+    exchange = functools.partial(
+        lax.all_to_all,
+        axis_name=("fsdp", "expert"),
+        split_axis=0,
+        concat_axis=0,
+        tiled=True,
+        axis_index_groups=groups,
+    )
     count, width = tokens.shape
     capacity = 3 * count // (2 * experts)
     weights = lax.all_gather(join(up_weight, down_weight), "fsdp", axis=0, tiled=True)
-    send, mix, own = dispatch(expert_ids.T, gate_probs.T, tokens, out_grad, experts, capacity)
-    recv = lax.all_to_all(send, "expert", split_axis=0, concat_axis=0, tiled=True)
+    places = place_in_order(expert_ids.T, side, lax.axis_index("fsdp") % 2)
+    send, mix, own = dispatch(places, gate_probs.T, tokens, out_grad, experts, capacity)
+    recv = exchange(send)
     x, g = unpack(recv.reshape(4 * experts * capacity, width // 2), capacity)
     packed = expert(x, g, weights, capacity)
-    back = lax.all_to_all(
-        packed.reshape(experts, 2 * capacity, width // 2 + 128),
-        "expert",
-        split_axis=0,
-        concat_axis=0,
-        tiled=True,
-    )
+    back = exchange(packed.reshape(experts, 2 * capacity, width // 2 + 128))
     d_tokens, d_gates = combine(back.reshape(packed.shape), mix.reshape(4 * count, -1), own)
     return d_tokens, d_gates.T
 

time: 151 us -> 151 us (level)
  transfers between devices with their start and end apart: 1 -> 1, of which waited for: 1 -> 1; matrix products, arithmetic and copies ran while one was open for 0% -> 1% of each run, Pallas kernels for 6% -> 6%
where the time goes in v3:
time: 151 us
  blocking collectives  72.7 us (48%)
  waiting for transfers between devices  41 us (27%)
  Pallas kernels  21.6 us (14%)
  between operations  14.1 us (9%)
    all_to_all x1, blocking collectives, body(): recv = exchange(send)  43.4 us
    all_gather x1, waiting for transfers between devices, body(): lax.all_gather(join(up_weight, down_weight), 'fsdp', axis=0, tiled=True)  40.9 us
    all_to_all x1, blocking collectives, body(): back = exchange(packed.reshape(experts, 2 * capacity, width // 2 + 128))  29.3 us
    pallas_call x1, Pallas kernels, expert(): pl.pallas_call(functools.partial(expert_kernel, capacity, cuts), in_specs...  8.87 us
    pallas_call x1, Pallas kernels, dispatch(): pl.pallas_call(functools.partial(dispatch_kernel, experts, capacity), gri...  5.71 us
  transfers between devices with their start and end apart: 1, of which 1 were waited for; matrix products, arithmetic and copies ran while one was open for 1% of the time, Pallas kernels for 6%

profile of v3, /device:TPU:1, one launch (start us, length us, event | category | flops | bytes accessed | tf_op | source)
XLA Modules:
  0.0 150.6 jit_solution(8176301104140392579)
XLA Ops:
  7.2 0.0 all-gather.2.cloned.1.call-start
  7.2 1.9 %join.1 = bf16[128,1536]{1,0:T(8,128)(2,1)} custom-call(bf16[1,128,768]{2,1,0:T(8,128)(2,1)} %up_ref.1, bf16[1,768,128]{2,1,0:T(8,128)(2,1)} %down_ref.1), custom_call_target="tpu_custom_call" | custom-call | tf_op jit(solution)/shard_map/join/pallas_call | solution.py:235
  9.1 0.0 all-gather.2.cloned.1.call-update
  9.1 1.2 fusion.1.ids_ref
  10.3 5.7 %dispatch.1 = (bf16[16,48,2048]{2,1,0:T(8,128)(2,1)}, bf16[2,2,128,384]{3,2,1,0:T(8,128)(2,1)}, bf16[2,384,128]{2,1,0:T(8,128)(2,1)}) custom-call(s32[2,128]{1,0:T(2,128)} %fusion.1.ids_ref, f32[2,128]{1,0:T(2,128)} %bitcast.24, bf16[128,4096]{1,0:T(8,128)(2,1)} %th.1, bf16[128,4096]{1,0:T(8,128)(2,1)} %th.1, bf16[128,4096]{1,0:T(8,128)(2,1)} %gh.1, ...), custom_call_target="tpu_custom_call" | custom-call | tf_op jit(solution)/shard_map/dispatch/pallas_call | solution.py:83
  16.1 43.4 %all_to_all.10 = bf16[16,48,2048]{2,1,0:T(8,128)(2,1)S(1)} all-to-all(bf16[16,48,2048]{2,1,0:T(8,128)(2,1)} %get-tuple-element.9), channel_id=1, replica_groups={{0,5,10,15,4,9,14,3,8,13,2,7,12,1,6,11},{16,21,26,31,17,22,27,28,18,23,..., dimensions={0} | all-to-all | bytes 6291456 | tf_op jit(solution)/shard_map/all_to_all | solution.py:274
  59.4 2.6 %unpack.1 = (bf16[192,4096]{1,0:T(8,128)(2,1)S(1)}, bf16[192,4096]{1,0:T(8,128)(2,1)S(1)}) custom-call(bf16[768,2048]{1,0:T(8,128)(2,1)S(1)} %bitcast.20), custom_call_target="tpu_custom_call" | custom-call | tf_op jit(solution)/shard_map/unpack/pallas_call | solution.py:124
  62.1 40.9 %all-gather.2.cloned.1.call-done.w_hbm = bf16[4096,1536]{1,0:T(8,128)(2,1)} async-done(((bf16[128,1536]{1,0:T(8,128)(2,1)}), bf16[4096,1536]{1,0:T(8,128)(2,1)}) %all-gather.2.cloned.1.call-update) | async-done | bytes 12582928 | tf_op jit(solution)/shard_map/all_gather | solution.py:271
  103.0 8.9 %expert.1 = bf16[384,2176]{1,0:T(8,128)(2,1)S(1)} custom-call(bf16[192,4096]{1,0:T(8,128)(2,1)S(1)} %get-tuple-element.10.x_ref, bf16[192,4096]{1,0:T(8,128)(2,1)S(1)} %get-tuple-element.11.g_ref, bf16[4096,1536]{1,0:T(8,128)(2,1)} %all-gather.2.cloned.1.call-done.w_hbm), custom_call_target="tpu_custom_call" | custom-call | tf_op jit(solution)/shard_map/expert/pallas_call | solution.py:171
  111.9 0.0 copy-start
  111.9 0.0 copy-start.1
  111.9 29.3 %all_to_all.11 = bf16[16,24,2176]{2,1,0:T(8,128)(2,1)S(1)} all-to-all(bf16[16,24,2176]{2,1,0:T(8,128)(2,1)S(1)} %bitcast.21), channel_id=1, replica_groups={{0,5,10,15,4,9,14,3,8,13,2,7,12,1,6,11},{16,21,26,31,17,22,27,28,18,23,..., dimensions={0} | all-to-all | bytes 3342336 | tf_op jit(solution)/shard_map/all_to_all | solution.py:277
  141.2 0.0 copy-done
  141.2 0.0 copy-done.1
  141.2 2.5 %combine.1 = (bf16[128,4096]{1,0:T(8,128)(2,1)}, bf16[2,128]{1,0:T(2,128)(2,1)}) custom-call(bf16[384,2176]{1,0:T(8,128)(2,1)S(1)} %bitcast.22, bf16[512,384]{1,0:T(8,128)(2,1)S(1)} %bitcast.23, bf16[2,384,128]{2,1,0:T(8,128)(2,1)S(1)} %copy-done.1), custom_call_target="tpu_custom_call" | custom-call | tf_op jit(solution)/shard_map/combine/pallas_call | solution.py:211
Async XLA Ops:
  7.2 95.8 %all-gather.2.cloned.1.call-start = ((), (), s32[]{:S(2)}) async-start(), calls=%async_computation.2 | async-start | bytes 12976128 | tf_op jit(solution)/shard_map/all_gather | solution.py:271
  111.9 29.3 %copy-start = (bf16[2,2,128,384]{3,2,1,0:T(8,128)(2,1)S(1)}, bf16[2,2,128,384]{3,2,1,0:T(8,128)(2,1)}, u32[]{:S(2)}) copy-start(bf16[2,2,128,384]{3,2,1,0:T(8,128)(2,1)} %get-tuple-element.12) | copy-start | bytes 1179652
  111.9 29.3 %copy-start.1 = (bf16[2,384,128]{2,1,0:T(8,128)(2,1)S(1)}, bf16[2,384,128]{2,1,0:T(8,128)(2,1)}, u32[]{:S(2)}) copy-start(bf16[2,384,128]{2,1,0:T(8,128)(2,1)} %get-tuple-element.13.own_ref) | copy-start | bytes 589828
Sparse Core Ops, SparseCore 0:
  10.1 92.8 all-gather.1

commit v4 on v3

--- a/solution.py
+++ b/solution.py
@@ -10,6 +10,7 @@
 
 F32, BF16 = jnp.float32, jnp.bfloat16
 VMEM_LIMIT = 56 * 1024 * 1024
+HEAD = 8
 
 
 def dot(left, right):
@@ -58,13 +59,24 @@
         weight = jnp.where(expert == ids[0:1, :], gates[0:1, :], gates[1:2, :])
         coarse = weight.astype(BF16)
         fine = (weight - coarse.astype(F32)).astype(BF16)
+        short = experts * HEAD
+        tail = capacity - HEAD
+        spread = (iota((short, experts), 0) // HEAD == iota((short, experts), 1)).astype(F32).astype(BF16)
+        place = iota((short, tokens), 0) % HEAD
+        slot = dot(spread, table.astype(BF16)).astype(jnp.int32)
+        whole = slot == place
+        sides = ((place < tail) & (slot == HEAD + place), (place >= tail) & (slot == HEAD + place - tail))
         for part, value in enumerate((coarse, fine)):
             wide = dot(spread, value)
-            for half, chosen in enumerate((low, high)):
-                mix_ref[half, part] = jnp.where(chosen, wide, 0.0).T.astype(BF16)
-        whose = iota((count, tokens), 0) // rows
+            lines = slice(part * tokens, (part + 1) * tokens)
+            for half, chosen in enumerate(sides):
+                mix_ref[half, lines, :short] = jnp.where(whole, wide, 0.0).T.astype(BF16)
+                mix_ref[half, lines, short:] = jnp.where(chosen, wide, 0.0).T.astype(BF16)
+        whose = iota((short, tokens), 0) // HEAD
         for choice in range(2):
-            own_ref[choice] = (low & (whose == ids[choice : choice + 1, :])).astype(F32).astype(BF16)
+            mine = whose == ids[choice : choice + 1, :]
+            own_ref[choice, :short] = (whole & mine).astype(F32).astype(BF16)
+            own_ref[choice, short:] = (sides[0] & mine).astype(F32).astype(BF16)
 
     count = experts * rows
     width = send_ref.shape[2]
@@ -86,13 +98,13 @@
         in_specs=[whole(ids.shape), whole(gates.shape), low, high, low, high],
         out_specs=[
             pl.BlockSpec((experts, 2 * rows, block), lambda i: (0, 0, i)),
-            whole((2, 2, count, experts * rows)),
-            whole((2, experts * rows, count)),
+            whole((2, 2 * count, 2 * experts * HEAD)),
+            whole((2, 2 * experts * HEAD, count)),
         ],
         out_shape=[
             jax.ShapeDtypeStruct((experts, 2 * rows, width // 2), BF16),
-            jax.ShapeDtypeStruct((2, 2, count, experts * rows), BF16),
-            jax.ShapeDtypeStruct((2, experts * rows, count), BF16),
+            jax.ShapeDtypeStruct((2, 2 * count, 2 * experts * HEAD), BF16),
+            jax.ShapeDtypeStruct((2, 2 * experts * HEAD, count), BF16),
         ],
         scratch_shapes=[pltpu.VMEM((2, experts * rows, count), BF16)],
         compiler_params=params("arbitrary"),
@@ -108,7 +120,11 @@
     slots, width = tokens_ref.shape
     total, half = recv_ref.shape
     row, column = iota((slots, total), 0), iota((slots, total), 1)
-    base = (row // capacity) * (4 * capacity) + row % capacity
+    tail = capacity - HEAD
+    first = HEAD * slots // capacity
+    source = jnp.where(row < first, row // HEAD, (row - first) // tail)
+    slot = jnp.where(row < first, row % HEAD, HEAD + (row - first) % tail)
+    base = source * (4 * capacity) + slot
     block = half // 4
     for part, out in enumerate((tokens_ref, grads_ref)):
         for side in range(2):
@@ -131,20 +147,23 @@
     )(recv)
 
 
-def expert_kernel(capacity, cuts, x_ref, g_ref, w_hbm, out_ref, w, arrived):
-    slots, width = x_ref.shape
+def fold(left, right):
+    rows, width = left.shape
+    left, right = left.reshape(rows // 8, 8, width), right.reshape(rows // 8, 8, width)
+    upper = iota(left.shape, 1) < 4
+    even = jnp.where(upper, left, pltpu.roll(right, 4, 1))
+    odd = jnp.where(upper, pltpu.roll(left, 4, 1), right)
+    return jnp.stack([even, odd], axis=1).reshape(2 * rows, width)
+
+
+def expert_kernel(cuts, x_ref, g_ref, w_hbm, out_ref, w, arrived):
+    width = x_ref.shape[1]
     wide = w.shape[1] // 2
     loads = []
     for i in range(len(cuts) - 1):
         part = pl.ds(cuts[i], cuts[i + 1] - cuts[i])
         loads.append(pltpu.make_async_copy(w_hbm.at[part], w.at[part], arrived.at[i]))
         loads[i].start()
-    rows = 2 * capacity
-    row, column = iota((2 * slots, slots), 0), iota((2 * slots, slots), 1)
-    base = (row // rows) * capacity + row % rows
-    low = (column == base) & (row % rows < capacity)
-    high = (column == base - capacity) & (row % rows >= capacity)
-    low, high = low.astype(F32).astype(BF16), high.astype(F32).astype(BF16)
     h = a = None
     for i in range(len(cuts) - 1):
         loads[i].wait()
@@ -154,25 +173,30 @@
     cdf = 0.5 * (1.0 + lax.erf(h * 0.7071067811865476))
     density = jnp.exp(-0.5 * h * h) * 0.3989422804014327
     active = (h * cdf).astype(BF16).astype(F32)
-    gate = jnp.sum(active * a, axis=1, keepdims=True).astype(BF16)
+    gate = jnp.sum(active * a, axis=1, keepdims=True)
     hidden_grad = (a * (cdf + h * density)).astype(BF16)
+    first = out_ref.shape[0]
     half = width // 2
     block = half // 4
     for i in range(4):
-        left = dot_t(hidden_grad, w[i * block : (i + 1) * block, :wide]).astype(BF16)
-        right = dot_t(hidden_grad, w[half + i * block : half + (i + 1) * block, :wide]).astype(BF16)
-        out_ref[:, i * block : (i + 1) * block] = (dot(low, left) + dot(high, right)).astype(BF16)
-    out_ref[:, half:] = dot(low, jnp.broadcast_to(gate, (slots, 128))).astype(BF16)
+        left = dot_t(hidden_grad, w[i * block : (i + 1) * block, :wide])
+        right = dot_t(hidden_grad, w[half + i * block : half + (i + 1) * block, :wide])
+        out_ref[:, i * block : (i + 1) * block] = left[:first].astype(BF16)
+        out_ref[:, half + i * block : half + (i + 1) * block] = right[:first].astype(BF16)
+        out_ref[:, width + i * block : width + (i + 1) * block] = fold(left[first:], right[first:]).astype(BF16)
+    lanes = jnp.broadcast_to(gate, (gate.shape[0], 128))
+    rest = fold(lanes[first:], lanes[first:])
+    out_ref[:, width + half :] = jnp.where(iota(rest.shape, 1) < 64, lanes[:first], rest).astype(BF16)
 
 
 def expert(x, g, weights, capacity):
     slots, width = x.shape
     cuts = tuple(width * eighth // 8 for eighth in (0, 1, 2, 4, 6, 8))
     return pl.pallas_call(
-        functools.partial(expert_kernel, capacity, cuts),
+        functools.partial(expert_kernel, cuts),
         in_specs=[IN_VMEM, IN_VMEM, IN_HBM],
         out_specs=IN_VMEM,
-        out_shape=jax.ShapeDtypeStruct((2 * slots, width // 2 + 128), BF16),
+        out_shape=jax.ShapeDtypeStruct((HEAD * slots // capacity, 3 * width // 2 + 128), BF16),
         scratch_shapes=[
             pltpu.VMEM(weights.shape, BF16),
             pltpu.SemaphoreType.DMA((len(cuts) - 1,)),
@@ -188,15 +212,17 @@
     block = half // blocks
     stores = []
     for i in range(blocks):
-        total = dot(mix_ref[...], back_ref[:, i * block : (i + 1) * block])
+        rest = back_ref[:, width + i * block : width + (i + 1) * block]
         for side in range(2):
-            coarse, fine = (total[(2 * side + j) * count : (2 * side + j + 1) * count] for j in range(2))
             start = side * half + i * block
-            out[:, start : start + block] = (coarse + fine).astype(BF16)
+            rows = jnp.concatenate([back_ref[:, start : start + block], rest], axis=0)
+            total = dot(mix_ref[side], rows)
+            out[:, start : start + block] = (total[:count] + total[count:]).astype(BF16)
             part = pl.ds(start, block)
             stores.append(pltpu.make_async_copy(out.at[:, part], tokens_hbm.at[:, part], left.at[2 * i + side]))
             stores[-1].start()
-    column = back_ref[:, half : half + 1].astype(F32)
+    lanes = back_ref[:, width + half :].astype(F32)
+    column = jnp.concatenate([lanes[:, 0:1], lanes[:, 64:65]], axis=0)
     for choice in range(2):
         picked = jnp.sum(own_ref[choice].astype(F32) * column, axis=0, keepdims=True)
         gates_ref[choice : choice + 1, :] = picked.astype(BF16)
@@ -204,8 +230,7 @@
         store.wait()
 
 
-def combine(back, mix, own):
-    half = back.shape[1] - 128
+def combine(back, mix, own, width):
     count = own.shape[2]
     blocks = 4
     return pl.pallas_call(
@@ -213,11 +238,11 @@
         in_specs=[IN_VMEM, IN_VMEM, IN_VMEM],
         out_specs=[IN_HBM, IN_VMEM],
         out_shape=[
-            jax.ShapeDtypeStruct((count, 2 * half), BF16),
+            jax.ShapeDtypeStruct((count, width), BF16),
             jax.ShapeDtypeStruct((2, count), BF16),
         ],
         scratch_shapes=[
-            pltpu.VMEM((count, 2 * half), BF16),
+            pltpu.VMEM((count, width), BF16),
             pltpu.SemaphoreType.DMA((2 * blocks,)),
         ],
         compiler_params=pltpu.CompilerParams(vmem_limit_bytes=16 * 1024 * 1024),
@@ -274,8 +299,8 @@
     recv = exchange(send)
     x, g = unpack(recv.reshape(4 * experts * capacity, width // 2), capacity)
     packed = expert(x, g, weights, capacity)
-    back = exchange(packed.reshape(experts, 2 * capacity, width // 2 + 128))
-    d_tokens, d_gates = combine(back.reshape(packed.shape), mix.reshape(4 * count, -1), own)
+    back = exchange(packed.reshape(experts, HEAD, -1))
+    d_tokens, d_gates = combine(back.reshape(packed.shape), mix, own, width)
     return d_tokens, d_gates.T
 
 

time: 151 us -> 149 us (0.987)
  Pallas kernels: 21.6 us -> 19.6 us
where the time goes in v4:
time: 149 us
  blocking collectives  72.1 us (48%)
  waiting for transfers between devices  41.8 us (28%)
  Pallas kernels  19.6 us (13%)
  between operations  14.1 us (9%)
    all_to_all x1, blocking collectives, body(): recv = exchange(send)  43.4 us
    all_gather x1, waiting for transfers between devices, body(): lax.all_gather(join(up_weight, down_weight), 'fsdp', axis=0, tiled=True)  41.8 us
    all_to_all x1, blocking collectives, body(): back = exchange(packed.reshape(experts, HEAD, -1))  28.7 us
    pallas_call x1, Pallas kernels, expert(): pl.pallas_call(functools.partial(expert_kernel, cuts), in_specs=[IN_VMEM,...  7.54 us
    pallas_call x1, Pallas kernels, dispatch(): pl.pallas_call(functools.partial(dispatch_kernel, experts, capacity), gri...  5.63 us
  transfers between devices with their start and end apart: 1, of which 1 were waited for; matrix products, arithmetic and copies ran while one was open for 1% of the time, Pallas kernels for 6%

profile of v4, /device:TPU:1, one launch (start us, length us, event | category | flops | bytes accessed | tf_op | source)
XLA Modules:
  0.0 148.8 jit_solution(3890124277552354183)
XLA Ops:
  7.2 0.0 all-gather.2.cloned.1.call-start
  7.2 1.9 %join.1 = bf16[128,1536]{1,0:T(8,128)(2,1)} custom-call(bf16[1,128,768]{2,1,0:T(8,128)(2,1)} %up_ref.1, bf16[1,768,128]{2,1,0:T(8,128)(2,1)} %down_ref.1), custom_call_target="tpu_custom_call" | custom-call | tf_op jit(solution)/shard_map/join/pallas_call | solution.py:260
  9.1 0.0 all-gather.2.cloned.1.call-update
  9.1 1.2 fusion.1.ids_ref
  10.3 5.6 %dispatch.1 = (bf16[16,48,2048]{2,1,0:T(8,128)(2,1)}, bf16[2,256,256]{2,1,0:T(8,128)(2,1)}, bf16[2,256,128]{2,1,0:T(8,128)(2,1)}) custom-call(s32[2,128]{1,0:T(2,128)} %fusion.1.ids_ref, f32[2,128]{1,0:T(2,128)} %bitcast.22, bf16[128,4096]{1,0:T(8,128)(2,1)} %th.1, bf16[128,4096]{1,0:T(8,128)(2,1)} %th.1, bf16[128,4096]{1,0:T(8,128)(2,1)} %gh.1, ...), custom_call_target="tpu_custom_call" | custom-call | tf_op jit(solution)/shard_map/dispatch/pallas_call | solution.py:95
  16.0 43.4 %all_to_all.10 = bf16[16,48,2048]{2,1,0:T(8,128)(2,1)S(1)} all-to-all(bf16[16,48,2048]{2,1,0:T(8,128)(2,1)} %get-tuple-element.9), channel_id=1, replica_groups={{0,5,10,15,4,9,14,3,8,13,2,7,12,1,6,11},{16,21,26,31,17,22,27,28,18,23,..., dimensions={0} | all-to-all | bytes 6291456 | tf_op jit(solution)/shard_map/all_to_all | solution.py:299
  59.3 2.6 %unpack.1 = (bf16[192,4096]{1,0:T(8,128)(2,1)S(1)}, bf16[192,4096]{1,0:T(8,128)(2,1)S(1)}) custom-call(bf16[768,2048]{1,0:T(8,128)(2,1)S(1)} %bitcast.19), custom_call_target="tpu_custom_call" | custom-call | tf_op jit(solution)/shard_map/unpack/pallas_call | solution.py:140
  62.0 41.8 %all-gather.2.cloned.1.call-done.w_hbm = bf16[4096,1536]{1,0:T(8,128)(2,1)} async-done(((bf16[128,1536]{1,0:T(8,128)(2,1)}), bf16[4096,1536]{1,0:T(8,128)(2,1)}) %all-gather.2.cloned.1.call-update) | async-done | bytes 12582928 | tf_op jit(solution)/shard_map/all_gather | solution.py:296
  103.7 7.5 %expert.1 = bf16[128,6272]{1,0:T(8,128)(2,1)S(1)} custom-call(bf16[192,4096]{1,0:T(8,128)(2,1)S(1)} %get-tuple-element.10.x_ref, bf16[192,4096]{1,0:T(8,128)(2,1)S(1)} %get-tuple-element.11.g_ref, bf16[4096,1536]{1,0:T(8,128)(2,1)} %all-gather.2.cloned.1.call-done.w_hbm), custom_call_target="tpu_custom_call" | custom-call | tf_op jit(solution)/shard_map/expert/pallas_call | solution.py:195
  111.3 0.0 copy-start
  111.3 0.0 copy-start.1
  111.3 28.7 %all_to_all.11 = bf16[16,8,6272]{2,1,0:T(8,128)(2,1)S(1)} all-to-all(bf16[16,8,6272]{2,1,0:T(8,128)(2,1)S(1)} %bitcast.20), channel_id=1, replica_groups={{0,5,10,15,4,9,14,3,8,13,2,7,12,1,6,11},{16,21,26,31,17,22,27,28,18,23,..., dimensions={0} | all-to-all | bytes 3211264 | tf_op jit(solution)/shard_map/all_to_all | solution.py:302
  140.0 0.0 copy-done
  140.0 0.0 copy-done.1
  140.0 1.9 %combine.1 = (bf16[128,4096]{1,0:T(8,128)(2,1)}, bf16[2,128]{1,0:T(2,128)(2,1)}) custom-call(bf16[128,6272]{1,0:T(8,128)(2,1)S(1)} %bitcast.21, bf16[2,256,256]{2,1,0:T(8,128)(2,1)S(1)} %copy-done, bf16[2,256,128]{2,1,0:T(8,128)(2,1)S(1)} %copy-done.1), custom_call_target="tpu_custom_call" | custom-call | tf_op jit(solution)/shard_map/combine/pallas_call | solution.py:236
Async XLA Ops:
  7.2 96.5 %all-gather.2.cloned.1.call-start = ((), (), s32[]{:S(2)}) async-start(), calls=%async_computation.2 | async-start | bytes 12976128 | tf_op jit(solution)/shard_map/all_gather | solution.py:296
  111.3 28.7 %copy-start = (bf16[2,256,256]{2,1,0:T(8,128)(2,1)S(1)}, bf16[2,256,256]{2,1,0:T(8,128)(2,1)}, u32[]{:S(2)}) copy-start(bf16[2,256,256]{2,1,0:T(8,128)(2,1)} %get-tuple-element.12.mix_ref) | copy-start | bytes 786436
  111.3 28.7 %copy-start.1 = (bf16[2,256,128]{2,1,0:T(8,128)(2,1)S(1)}, bf16[2,256,128]{2,1,0:T(8,128)(2,1)}, u32[]{:S(2)}) copy-start(bf16[2,256,128]{2,1,0:T(8,128)(2,1)} %get-tuple-element.13.own_ref) | copy-start | bytes 393220
Sparse Core Ops, SparseCore 0:
  10.7 92.9 all-gather.1

commit v5 on v4

--- a/solution.py
+++ b/solution.py
@@ -267,14 +267,12 @@
 
 
 def exchange_orders(side):
-    first = [((i % side + i // side) % side) * side + i % side for i in range(side * side)]
+    first = list(range(side * side))
     return first, [(device % side) * side + device // side for device in first]
 
 
 def place_in_order(ids, side, core):
-    x, y = ids // side, ids % side
-    along, across = jnp.where(core == 0, x, y), jnp.where(core == 0, y, x)
-    return ((along - across) % side) * side + across
+    return jnp.where(core == 0, ids, (ids % side) * side + ids // side)
 
 
 def body(tokens, expert_ids, gate_probs, up_weight, down_weight, out_grad):

time: 149 us -> 149 us (level)
  no operation moved by 1% of the time
where the time goes in v5:
time: 149 us
  blocking collectives  73.5 us (49%)
  waiting for transfers between devices  40.5 us (27%)
  Pallas kernels  19.6 us (13%)
  between operations  14.1 us (9%)
    all_to_all x1, blocking collectives, body(): recv = exchange(send)  44.5 us
    all_gather x1, waiting for transfers between devices, body(): lax.all_gather(join(up_weight, down_weight), 'fsdp', axis=0, tiled=True)  40.5 us
    all_to_all x1, blocking collectives, body(): back = exchange(packed.reshape(experts, HEAD, -1))  29 us
    pallas_call x1, Pallas kernels, expert(): pl.pallas_call(functools.partial(expert_kernel, cuts), in_specs=[IN_VMEM,...  7.55 us
    pallas_call x1, Pallas kernels, dispatch(): pl.pallas_call(functools.partial(dispatch_kernel, experts, capacity), gri...  5.63 us
  transfers between devices with their start and end apart: 1, of which 1 were waited for; matrix products, arithmetic and copies ran while one was open for 1% of the time, Pallas kernels for 6%

profile of v5, /device:TPU:1, one launch (start us, length us, event | category | flops | bytes accessed | tf_op | source)
XLA Modules:
  0.0 148.9 jit_solution(9748867752111227625)
XLA Ops:
  7.2 0.0 all-gather.2.cloned.1.call-start
  7.2 1.9 %join.1 = bf16[128,1536]{1,0:T(8,128)(2,1)} custom-call(bf16[1,128,768]{2,1,0:T(8,128)(2,1)} %up_ref.1, bf16[1,768,128]{2,1,0:T(8,128)(2,1)} %down_ref.1), custom_call_target="tpu_custom_call" | custom-call | tf_op jit(solution)/shard_map/join/pallas_call | solution.py:260
  9.1 0.0 all-gather.2.cloned.1.call-update
  9.1 1.2 fusion.2.ids_ref
  10.3 5.6 %dispatch.1 = (bf16[16,48,2048]{2,1,0:T(8,128)(2,1)}, bf16[2,256,256]{2,1,0:T(8,128)(2,1)}, bf16[2,256,128]{2,1,0:T(8,128)(2,1)}) custom-call(s32[2,128]{1,0:T(2,128)} %fusion.2.ids_ref, f32[2,128]{1,0:T(2,128)} %bitcast.16, bf16[128,4096]{1,0:T(8,128)(2,1)} %th.1, bf16[128,4096]{1,0:T(8,128)(2,1)} %th.1, bf16[128,4096]{1,0:T(8,128)(2,1)} %gh.1, ...), custom_call_target="tpu_custom_call" | custom-call | tf_op jit(solution)/shard_map/dispatch/pallas_call | solution.py:95
  16.0 44.5 %all_to_all.10 = bf16[16,48,2048]{2,1,0:T(8,128)(2,1)S(1)} all-to-all(bf16[16,48,2048]{2,1,0:T(8,128)(2,1)} %get-tuple-element.9), channel_id=1, replica_groups={{0,1,2,3,4,5,6,7,8,9,10,11,12,13,14,15},{16,20,24,28,17,21,25,29,18,22,..., dimensions={0} | all-to-all | bytes 6291456 | tf_op jit(solution)/shard_map/all_to_all | solution.py:297
  60.5 2.6 %unpack.1 = (bf16[192,4096]{1,0:T(8,128)(2,1)S(1)}, bf16[192,4096]{1,0:T(8,128)(2,1)S(1)}) custom-call(bf16[768,2048]{1,0:T(8,128)(2,1)S(1)} %bitcast.13), custom_call_target="tpu_custom_call" | custom-call | tf_op jit(solution)/shard_map/unpack/pallas_call | solution.py:140
  63.1 40.5 %all-gather.2.cloned.1.call-done.w_hbm = bf16[4096,1536]{1,0:T(8,128)(2,1)} async-done(((bf16[128,1536]{1,0:T(8,128)(2,1)}), bf16[4096,1536]{1,0:T(8,128)(2,1)}) %all-gather.2.cloned.1.call-update) | async-done | bytes 12582928 | tf_op jit(solution)/shard_map/all_gather | solution.py:294
  103.6 7.5 %expert.1 = bf16[128,6272]{1,0:T(8,128)(2,1)S(1)} custom-call(bf16[192,4096]{1,0:T(8,128)(2,1)S(1)} %get-tuple-element.10.x_ref, bf16[192,4096]{1,0:T(8,128)(2,1)S(1)} %get-tuple-element.11.g_ref, bf16[4096,1536]{1,0:T(8,128)(2,1)} %all-gather.2.cloned.1.call-done.w_hbm), custom_call_target="tpu_custom_call" | custom-call | tf_op jit(solution)/shard_map/expert/pallas_call | solution.py:195
  111.1 0.0 copy-start
  111.2 0.0 copy-start.1
  111.2 29.0 %all_to_all.11 = bf16[16,8,6272]{2,1,0:T(8,128)(2,1)S(1)} all-to-all(bf16[16,8,6272]{2,1,0:T(8,128)(2,1)S(1)} %bitcast.14), channel_id=1, replica_groups={{0,1,2,3,4,5,6,7,8,9,10,11,12,13,14,15},{16,20,24,28,17,21,25,29,18,22,..., dimensions={0} | all-to-all | bytes 3211264 | tf_op jit(solution)/shard_map/all_to_all | solution.py:300
  140.1 0.0 copy-done
  140.1 0.0 copy-done.1
  140.1 1.9 %combine.1 = (bf16[128,4096]{1,0:T(8,128)(2,1)}, bf16[2,128]{1,0:T(2,128)(2,1)}) custom-call(bf16[128,6272]{1,0:T(8,128)(2,1)S(1)} %bitcast.15, bf16[2,256,256]{2,1,0:T(8,128)(2,1)S(1)} %copy-done, bf16[2,256,128]{2,1,0:T(8,128)(2,1)S(1)} %copy-done.1), custom_call_target="tpu_custom_call" | custom-call | tf_op jit(solution)/shard_map/combine/pallas_call | solution.py:236
Async XLA Ops:
  7.2 96.4 %all-gather.2.cloned.1.call-start = ((), (), s32[]{:S(2)}) async-start(), calls=%async_computation.2 | async-start | bytes 12976128 | tf_op jit(solution)/shard_map/all_gather | solution.py:294
  111.1 29.0 %copy-start = (bf16[2,256,256]{2,1,0:T(8,128)(2,1)S(1)}, bf16[2,256,256]{2,1,0:T(8,128)(2,1)}, u32[]{:S(2)}) copy-start(bf16[2,256,256]{2,1,0:T(8,128)(2,1)} %get-tuple-element.12.mix_ref) | copy-start | bytes 786436
  111.2 29.0 %copy-start.1 = (bf16[2,256,128]{2,1,0:T(8,128)(2,1)S(1)}, bf16[2,256,128]{2,1,0:T(8,128)(2,1)}, u32[]{:S(2)}) copy-start(bf16[2,256,128]{2,1,0:T(8,128)(2,1)} %get-tuple-element.13.own_ref) | copy-start | bytes 393220
Sparse Core Ops, SparseCore 0:
  10.7 92.8 all-gather.1
